TPU v7x, 256 devices: a whole 4x4x8 slice. The times are simulated.
256 devices in a mesh: slide: 8 (over x, core), seq: 32 (over y, z).
Axes of the slice: x: 4, y: 4, z: 8, core: 2. Of those that a mesh axis runs over, the one named last changes fastest.
Arguments:
- queries: bfloat16 [8, 8192, 1536], P('slide', 'seq'), may hold values from -9 to 9
- key_rows: bfloat16 [8, 8192, 1536], P('slide', 'seq'), may hold values from -9 to 9
- value_rows: bfloat16 [8, 8192, 1536], P('slide', 'seq'), may hold values from -12 to 12
- tissue: int32 [8, 8192], P('slide', 'seq'), may hold values from 0 to 1, as said below
- segment_len: int32 [24], replicated, may hold values from 128 to 256, as said below
- dilation: int32 [24], replicated, may hold values from 1 to 4, as said below
- out_weight: bfloat16 [1536, 1536], P(('slide', 'seq')), may hold values from -0.15625 to 0.15625
- grad_out: bfloat16 [8, 8192, 1536], P('slide', 'seq'), may hold values from -6 to 6
Outputs:
- layer_out: bfloat16 [8, 8192, 1536], P('slide', 'seq')
- grad_query: bfloat16 [8, 8192, 1536], P('slide', 'seq')
- grad_key: bfloat16 [8, 8192, 1536], P('slide', 'seq')
- grad_value: bfloat16 [8, 8192, 1536], P('slide', 'seq')
- grad_weight: float32 [1536, 1536], P(('slide', 'seq'))
Inputs may be any that keep to these rules, and one draw needn't show every extreme that they name: 1 for tissue, 0 for background. `segment_len`: each entry is 256 or 128, and each value is taken by some head. `dilation`: each entry is 1, 2 or 4; some head has 1 and some head 4.
All inputs are finite; a program needn't handle non-finite values.
Results may differ from a plain program's by a relative error of at most 0.0079.
Values may be sent and summed in bfloat16 or wider, within the bound.
A program may use at most 128 MiB of HBM per device.

v0:
```python
import math

import jax
import jax.numpy as jnp
from jax import lax
from jax.sharding import PartitionSpec as P

HD = 64


def heads_of(matrix):
    return matrix.reshape(matrix.shape[0], matrix.shape[1] // HD, HD)


def local_allowed(keep_row, segment_len, dilation):
    count = keep_row.shape[0]
    places = jnp.arange(count, dtype=jnp.int32)
    seg_col = segment_len[:, None, None]
    rate_col = dilation[:, None, None]
    row_pos = places[None, :, None]
    col_pos = places[None, None, :]
    inside = (row_pos // seg_col == col_pos // seg_col) & (row_pos % rate_col == col_pos % rate_col)
    inside = inside & (keep_row[None, None, :] == 1)
    return inside | (row_pos == col_pos)


def scores_of(q_heads, k_heads):
    return jnp.einsum(
        "ihd,jhd->hij", q_heads, k_heads, preferred_element_type=jnp.float32
    ) * HD ** (-0.5)


def forward_part(q_heads, k_heads, v_heads, allowed):
    scores = scores_of(q_heads, k_heads)
    top_all = jnp.max(jnp.where(allowed, scores, -1e30), axis=2)
    weights = jnp.where(allowed, jnp.exp(scores - top_all[:, :, None]), 0.0)
    totals = jnp.sum(weights, axis=2)
    summed = jnp.einsum(
        "hij,jhd->ihd", weights.astype(jnp.bfloat16), v_heads, preferred_element_type=jnp.float32
    )
    return (top_all, totals, summed)


def backward_part(q_heads, k_heads, v_heads, allowed, lse, delta, d_heads):
    scale = HD ** (-0.5)
    scores = scores_of(q_heads, k_heads)
    probs = jnp.where(allowed, jnp.exp(scores - lse[:, :, None]), 0.0)
    grad_v = jnp.einsum(
        "hij,ihd->jhd", probs.astype(jnp.bfloat16), d_heads, preferred_element_type=jnp.float32
    )
    dprob = jnp.einsum("ihd,jhd->hij", d_heads, v_heads, preferred_element_type=jnp.float32)
    dscore = (probs * (dprob - delta[:, :, None])).astype(jnp.bfloat16)
    grad_q = jnp.einsum("hij,jhd->ihd", dscore, k_heads, preferred_element_type=jnp.float32) * scale
    grad_k = jnp.einsum("hij,ihd->jhd", dscore, q_heads, preferred_element_type=jnp.float32) * scale
    return (grad_q, grad_k, grad_v)


def combine(m_near, l_near, m_far, l_far):
    top_all = jnp.maximum(m_near, m_far)
    scale_near = jnp.exp(m_near - top_all)
    scale_far = jnp.exp(m_far - top_all)
    totals = scale_near * l_near + scale_far * l_far
    return (top_all, scale_near, scale_far, totals)


def local(queries, key_rows, value_rows, tissue, segment_len, dilation, out_weight, grad_out):
    q_rows = queries[0]
    k_rows = key_rows[0]
    v_rows = value_rows[0]
    keep_row = tissue[0]
    upstream = grad_out[0]
    rows, features = q_rows.shape
    groups = lax.axis_size("seq")
    per_group = rows // groups

    def to_rows(matrix):
        return matrix.reshape((per_group, groups) + matrix.shape[1:])

    def from_rows(matrix):
        return matrix.reshape((rows,) + matrix.shape[2:])

    weight_full = lax.all_gather(out_weight, ("slide", "seq"), axis=0, tiled=True)
    d_attn = lax.dot_general(
        upstream, weight_full, (((1,), (1,)), ((), ())), preferred_element_type=jnp.float32
    ).astype(jnp.bfloat16)
    q_heads = heads_of(q_rows)
    k_heads = heads_of(k_rows)
    v_heads = heads_of(v_rows)
    d_heads = heads_of(d_attn)
    near_mask = local_allowed(keep_row, segment_len, dilation)
    m_near, l_near, acc_near = forward_part(q_heads, k_heads, v_heads, near_mask)
    g_near = jnp.sum(d_heads.astype(jnp.float32) * acc_near, axis=2).T
    moved = (
        lax.all_to_all(to_rows(q_rows), "seq", split_axis=1, concat_axis=0, tiled=True),
        lax.all_to_all(to_rows(k_rows), "seq", split_axis=1, concat_axis=0, tiled=True),
        lax.all_to_all(to_rows(v_rows), "seq", split_axis=1, concat_axis=0, tiled=True),
        lax.all_to_all(
            to_rows(keep_row.astype(jnp.bfloat16)), "seq", split_axis=1, concat_axis=0, tiled=True
        ),
        lax.all_to_all(to_rows(d_attn), "seq", split_axis=1, concat_axis=0, tiled=True),
    )
    qf_heads = heads_of(from_rows(moved[0]))
    kf_heads = heads_of(from_rows(moved[1]))
    vf_heads = heads_of(from_rows(moved[2]))
    far_mask = (from_rows(moved[3]) > 0.5)[None, None, :]
    df_heads = heads_of(from_rows(moved[4]))
    m_far, l_far, acc_far = forward_part(qf_heads, kf_heads, vf_heads, far_mask)
    g_far = jnp.sum(df_heads.astype(jnp.float32) * acc_far, axis=2).T
    back = (
        lax.all_to_all(
            acc_far.reshape(rows, 1, features), "seq", split_axis=0, concat_axis=1, tiled=True
        ),
        lax.all_to_all(m_far.T[:, None, :], "seq", split_axis=0, concat_axis=1, tiled=True),
        lax.all_to_all(l_far.T[:, None, :], "seq", split_axis=0, concat_axis=1, tiled=True),
        lax.all_to_all(g_far.T[:, None, :], "seq", split_axis=0, concat_axis=1, tiled=True),
    )
    acc_back = from_rows(back[0]).reshape(rows, features // HD, HD)
    m_back = from_rows(back[1]).T
    l_back = from_rows(back[2]).T
    g_back = from_rows(back[3]).T
    top_all, scale_near, scale_far, totals = combine(m_near, l_near, m_back, l_back)
    attn_f = (scale_near.T[:, :, None] * acc_near + scale_far.T[:, :, None] * acc_back) / totals.T[
        :, :, None
    ]
    attn = attn_f.reshape(rows, features).astype(jnp.bfloat16)
    lse = top_all + jnp.log(totals)
    delta = (scale_near * g_near + scale_far * g_back) / totals
    layer_out = jnp.dot(attn, weight_full, preferred_element_type=jnp.float32).astype(jnp.bfloat16)
    sent = (
        lax.all_to_all(to_rows(lse.T), "seq", split_axis=1, concat_axis=0, tiled=True),
        lax.all_to_all(to_rows(delta.T), "seq", split_axis=1, concat_axis=0, tiled=True),
    )
    lse_far = from_rows(sent[0]).T
    delta_far = from_rows(sent[1]).T
    gq_near, gk_near, gv_near = backward_part(
        q_heads, k_heads, v_heads, near_mask, lse, delta, d_heads
    )
    gq_far, gk_far, gv_far = backward_part(
        qf_heads, kf_heads, vf_heads, far_mask, lse_far, delta_far, df_heads
    )
    returned = (
        lax.all_to_all(
            gq_far.reshape(rows, 1, features).astype(jnp.bfloat16),
            "seq",
            split_axis=0,
            concat_axis=1,
            tiled=True,
        ),
        lax.all_to_all(
            gk_far.reshape(rows, 1, features).astype(jnp.bfloat16),
            "seq",
            split_axis=0,
            concat_axis=1,
            tiled=True,
        ),
        lax.all_to_all(
            gv_far.reshape(rows, 1, features).astype(jnp.bfloat16),
            "seq",
            split_axis=0,
            concat_axis=1,
            tiled=True,
        ),
    )
    grad_q = (gq_near.reshape(rows, features) + from_rows(returned[0]).astype(jnp.float32)).astype(
        jnp.bfloat16
    )
    grad_k = (gk_near.reshape(rows, features) + from_rows(returned[1]).astype(jnp.float32)).astype(
        jnp.bfloat16
    )
    grad_v = (gv_near.reshape(rows, features) + from_rows(returned[2]).astype(jnp.float32)).astype(
        jnp.bfloat16
    )
    share = lax.psum_scatter(
        lax.dot_general(
            attn, upstream, (((0,), (0,)), ((), ())), preferred_element_type=jnp.float32
        ),
        ("slide", "seq"),
        scatter_dimension=0,
        tiled=True,
    )
    factor = 1.0 / math.sqrt(lax.axis_size("slide") * lax.axis_size("seq") * rows)
    grad_weight = share * factor
    return (layer_out[None], grad_q[None], grad_k[None], grad_v[None], grad_weight)


def solution(mesh):
    placed = (
        P("slide", "seq", None),
        P("slide", "seq", None),
        P("slide", "seq", None),
        P("slide", "seq"),
        P(),
        P(),
        P(("slide", "seq"), None),
        P("slide", "seq", None),
    )
    return jax.shard_map(
        local,
        mesh=mesh,
        in_specs=placed,
        out_specs=(
            P("slide", "seq", None),
            P("slide", "seq", None),
            P("slide", "seq", None),
            P("slide", "seq", None),
            P(("slide", "seq"), None),
        ),
        check_vma=False,
    )
```

profile of v0, /device:TPU:2, one launch (start us, length us, event | category | flops | bytes accessed | tf_op | source)
XLA Modules:
  0.0 1709.6 jit_solution(16776777355466714787)
XLA Ops:
  35.9 21.0 %all-to-all-done.1 = bf16[8,32,1536]{2,0,1:T(8,128)(2,1)S(1)} async-done(((bf16[8,32,1536]{2,0,1:T(8,128)(2,1)}), bf16[8,32,1536]{2,0,1:T(8,128)(2,1)S(1)}, u32[]{:S(2)}, u32[]{:S(2)}) %all-to-all-start.1) | async-done | bytes 786464 | tf_op jit(solution)/shard_map/all_to_all | solution.py:94
  66.5 18.6 %all-to-all-done.2 = bf16[8,32,1536]{2,0,1:T(8,128)(2,1)S(1)} async-done(((bf16[8,32,1536]{2,0,1:T(8,128)(2,1)}), bf16[8,32,1536]{2,0,1:T(8,128)(2,1)S(1)}, u32[]{:S(2)}, u32[]{:S(2)}) %all-to-all-start.2) | async-done | bytes 786464 | tf_op jit(solution)/shard_map/all_to_all | solution.py:95
  187.7 13.5 all-to-all-done.7
  273.5 24.2 %all-to-all-done.5 = f32[256,1,1536]{2,1,0:T(1,128)} async-done(((f32[256,1,1536]{2,1,0:T(1,128)}), f32[256,1,1536]{2,1,0:T(1,128)}, u32[]{:S(2)}, u32[]{:S(2)}) %all-to-all-start.5) | async-done | bytes 1572896 | tf_op jit(solution)/shard_map/all_to_all | solution.py:110
  319.6 647.2 %fusion = f32[8,1536]{1,0:T(8,128)S(1)} fusion(f32[1536,1536]{1,0:T(8,128)} %fusion.41), kind=kCustom, calls=%all-reduce-scatter | all-reduce-scatter fusion | flops 3145729 | bytes 9486336
  974.9 68.4 %collective-permute-start.60 = (f32[8,1536]{1,0:T(8,128)S(1)}, f32[8,1536]{1,0:T(8,128)S(1)}, u32[]{:S(2)}, u32[]{:S(2)}) collective-permute-start(f32[8,1536]{1,0:T(8,128)S(1)} %fusion), channel_id=1, source_target_pairs={{0,61},{1,62},{2,63},{3,64},{4,65},{5,66},{6,67},{7,68},{8,69},{9,... | collective-permute-start | bytes 147464
  1185.3 13.1 collective-permute-start.27
  1198.5 13.1 collective-permute-start.26
  1211.6 13.1 collective-permute-start.25
  1234.2 13.2 collective-permute-start.24
  1247.4 13.1 collective-permute-start.23
  1260.6 13.1 collective-permute-start.22
  1273.7 13.1 collective-permute-start.21
  1286.9 13.1 collective-permute-start.20
  1303.0 13.1 collective-permute-start.19
  1316.1 13.1 collective-permute-start.18
  1329.3 13.1 collective-permute-start.17
  1342.4 13.1 collective-permute-start.16
  1373.2 13.1 collective-permute-start.14
  1386.4 13.1 collective-permute-start.13
  1399.5 13.1 collective-permute-start.12
  1412.7 13.1 collective-permute-start.11
  1425.8 13.1 collective-permute-start.10
  1467.2 13.1 collective-permute-start.8
  1480.3 13.1 collective-permute-start.7
  1493.5 13.1 collective-permute-start.6
  1521.1 13.1 collective-permute-start.4
  1534.2 13.1 collective-permute-start.3
  1547.4 13.1 collective-permute-start.2
  1560.5 13.1 collective-permute-start.1
  1574.3 13.1 collective-permute-start
  1596.1 97.1 %concatenate = f32[518,1536]{1,0:T(8,128)} concatenate(f32[6,1536]{1,0:T(8,128)S(1)} %copy-done.37, f32[8,1536]{1,0:T(8,128)S(1)} %copy-done.31, f32[8,1536]{1,0:T(8,128)S(1)} %copy-done.33, f32[8,1536]{1,0:T(8,128)S(1)} %copy-done.35, f32[8,1536]{1,0:T(8,128)S(1)} %copy-done.39, f32[8,1536]{1,0:T(8,128)S(1)} %copy-done.41, f32[8,1536]{1,0:T(8,128)S(1)} %copy-done.43, ...), dimensions={0} | concatenate | bytes 6365184
  (494 shorter events, 474.1 us)
Async XLA Ops:
  7.2 141.5 %all-gather.3.cloned.1.call-start = ((), (), s32[]{:S(2)}) async-start(), calls=%async_computation.14 | async-start | bytes 6316032 | tf_op jit(solution)/shard_map/all_gather | solution.py:82
  966.9 92.0 %collective-permute-start.62 = (f32[8,1536]{1,0:T(8,128)S(1)}, f32[8,1536]{1,0:T(8,128)S(1)}, u32[]{:S(2)}, u32[]{:S(2)}) collective-permute-start(f32[8,1536]{1,0:T(8,128)S(1)} %fusion), channel_id=1, source_target_pairs={{0,63},{1,64},{2,65},{3,66},{4,67},{5,68},{6,69},{7,70},{8,71},{9,... | collective-permute-start | bytes 147464
  973.0 87.8 %collective-permute-start.61 = (f32[8,1536]{1,0:T(8,128)S(1)}, f32[8,1536]{1,0:T(8,128)S(1)}, u32[]{:S(2)}, u32[]{:S(2)}) collective-permute-start(f32[8,1536]{1,0:T(8,128)S(1)} %fusion), channel_id=1, source_target_pairs={{0,62},{1,63},{2,64},{3,65},{4,66},{5,67},{6,68},{7,69},{8,70},{9,... | collective-permute-start | bytes 147464
  974.9 87.8 %collective-permute-start.60 = (f32[8,1536]{1,0:T(8,128)S(1)}, f32[8,1536]{1,0:T(8,128)S(1)}, u32[]{:S(2)}, u32[]{:S(2)}) collective-permute-start(f32[8,1536]{1,0:T(8,128)S(1)} %fusion), channel_id=1, source_target_pairs={{0,61},{1,62},{2,63},{3,64},{4,65},{5,66},{6,67},{7,68},{8,69},{9,... | collective-permute-start | bytes 147464
  1164.6 274.4 %all-to-all-start.11 = ((bf16[32,2,6144]{2,1,0:T(2,128)(2,1)}), bf16[32,2,6144]{2,1,0:T(2,128)(2,1)S(1)}, u32[]{:S(2)}, u32[]{:S(2)}) async-start(bf16[32,2,6144]{2,1,0:T(2,128)(2,1)} %reshape.574), calls=%async_computation.11 | async-start | bytes 1572864 | tf_op jit(solution)/shard_map/all_to_all | solution.py:142
  1169.2 65.0 %collective-permute-start.29 = (f32[8,1536]{1,0:T(8,128)S(1)}, f32[8,1536]{1,0:T(8,128)S(1)}, u32[]{:S(2)}, u32[]{:S(2)}) collective-permute-start(f32[8,1536]{1,0:T(8,128)S(1)} %fusion), channel_id=1, source_target_pairs={{0,30},{1,31},{2,32},{3,33},{4,34},{5,35},{6,36},{7,37},{8,38},{9,... | collective-permute-start | bytes 147464
  1177.2 70.2 %collective-permute-start.28 = (f32[8,1536]{1,0:T(8,128)S(1)}, f32[8,1536]{1,0:T(8,128)S(1)}, u32[]{:S(2)}, u32[]{:S(2)}) collective-permute-start(f32[8,1536]{1,0:T(8,128)S(1)} %fusion), channel_id=1, source_target_pairs={{0,29},{1,30},{2,31},{3,32},{4,33},{5,34},{6,35},{7,36},{8,37},{9,... | collective-permute-start | bytes 147464
  1185.3 75.2 %collective-permute-start.27 = (f32[8,1536]{1,0:T(8,128)S(1)}, f32[8,1536]{1,0:T(8,128)S(1)}, u32[]{:S(2)}, u32[]{:S(2)}) collective-permute-start(f32[8,1536]{1,0:T(8,128)S(1)} %fusion), channel_id=1, source_target_pairs={{0,28},{1,29},{2,30},{3,31},{4,32},{5,33},{6,34},{7,35},{8,36},{9,... | collective-permute-start | bytes 147464
  1198.5 75.2 %collective-permute-start.26 = (f32[8,1536]{1,0:T(8,128)S(1)}, f32[8,1536]{1,0:T(8,128)S(1)}, u32[]{:S(2)}, u32[]{:S(2)}) collective-permute-start(f32[8,1536]{1,0:T(8,128)S(1)} %fusion), channel_id=1, source_target_pairs={{0,27},{1,28},{2,29},{3,30},{4,31},{5,32},{6,33},{7,34},{8,35},{9,... | collective-permute-start | bytes 147464
  1211.6 75.2 %collective-permute-start.25 = (f32[8,1536]{1,0:T(8,128)S(1)}, f32[8,1536]{1,0:T(8,128)S(1)}, u32[]{:S(2)}, u32[]{:S(2)}) collective-permute-start(f32[8,1536]{1,0:T(8,128)S(1)} %fusion), channel_id=1, source_target_pairs={{0,26},{1,27},{2,28},{3,29},{4,30},{5,31},{6,32},{7,33},{8,34},{9,... | collective-permute-start | bytes 147464
  1234.2 68.8 %collective-permute-start.24 = (f32[8,1536]{1,0:T(8,128)S(1)}, f32[8,1536]{1,0:T(8,128)S(1)}, u32[]{:S(2)}, u32[]{:S(2)}) collective-permute-start(f32[8,1536]{1,0:T(8,128)S(1)} %fusion), channel_id=1, source_target_pairs={{0,25},{1,26},{2,27},{3,28},{4,29},{5,30},{6,31},{7,32},{8,33},{9,... | collective-permute-start | bytes 147464
  1247.4 68.7 %collective-permute-start.23 = (f32[8,1536]{1,0:T(8,128)S(1)}, f32[8,1536]{1,0:T(8,128)S(1)}, u32[]{:S(2)}, u32[]{:S(2)}) collective-permute-start(f32[8,1536]{1,0:T(8,128)S(1)} %fusion), channel_id=1, source_target_pairs={{0,24},{1,25},{2,26},{3,27},{4,28},{5,29},{6,30},{7,31},{8,32},{9,... | collective-permute-start | bytes 147464
  1260.6 68.7 %collective-permute-start.22 = (f32[8,1536]{1,0:T(8,128)S(1)}, f32[8,1536]{1,0:T(8,128)S(1)}, u32[]{:S(2)}, u32[]{:S(2)}) collective-permute-start(f32[8,1536]{1,0:T(8,128)S(1)} %fusion), channel_id=1, source_target_pairs={{0,23},{1,24},{2,25},{3,26},{4,27},{5,28},{6,29},{7,30},{8,31},{9,... | collective-permute-start | bytes 147464
  1273.7 68.7 %collective-permute-start.21 = (f32[8,1536]{1,0:T(8,128)S(1)}, f32[8,1536]{1,0:T(8,128)S(1)}, u32[]{:S(2)}, u32[]{:S(2)}) collective-permute-start(f32[8,1536]{1,0:T(8,128)S(1)} %fusion), channel_id=1, source_target_pairs={{0,22},{1,23},{2,24},{3,25},{4,26},{5,27},{6,28},{7,29},{8,30},{9,... | collective-permute-start | bytes 147464
  1286.9 68.7 %collective-permute-start.20 = (f32[8,1536]{1,0:T(8,128)S(1)}, f32[8,1536]{1,0:T(8,128)S(1)}, u32[]{:S(2)}, u32[]{:S(2)}) collective-permute-start(f32[8,1536]{1,0:T(8,128)S(1)} %fusion), channel_id=1, source_target_pairs={{0,21},{1,22},{2,23},{3,24},{4,25},{5,26},{6,27},{7,28},{8,29},{9,... | collective-permute-start | bytes 147464
  1303.0 70.3 %collective-permute-start.19 = (f32[8,1536]{1,0:T(8,128)S(1)}, f32[8,1536]{1,0:T(8,128)S(1)}, u32[]{:S(2)}, u32[]{:S(2)}) collective-permute-start(f32[8,1536]{1,0:T(8,128)S(1)} %fusion), channel_id=1, source_target_pairs={{0,20},{1,21},{2,22},{3,23},{4,24},{5,25},{6,26},{7,27},{8,28},{9,... | collective-permute-start | bytes 147464
  1316.1 70.3 %collective-permute-start.18 = (f32[8,1536]{1,0:T(8,128)S(1)}, f32[8,1536]{1,0:T(8,128)S(1)}, u32[]{:S(2)}, u32[]{:S(2)}) collective-permute-start(f32[8,1536]{1,0:T(8,128)S(1)} %fusion), channel_id=1, source_target_pairs={{0,19},{1,20},{2,21},{3,22},{4,23},{5,24},{6,25},{7,26},{8,27},{9,... | collective-permute-start | bytes 147464
  1329.3 70.3 %collective-permute-start.17 = (f32[8,1536]{1,0:T(8,128)S(1)}, f32[8,1536]{1,0:T(8,128)S(1)}, u32[]{:S(2)}, u32[]{:S(2)}) collective-permute-start(f32[8,1536]{1,0:T(8,128)S(1)} %fusion), channel_id=1, source_target_pairs={{0,18},{1,19},{2,20},{3,21},{4,22},{5,23},{6,24},{7,25},{8,26},{9,... | collective-permute-start | bytes 147464
  1342.4 70.3 %collective-permute-start.16 = (f32[8,1536]{1,0:T(8,128)S(1)}, f32[8,1536]{1,0:T(8,128)S(1)}, u32[]{:S(2)}, u32[]{:S(2)}) collective-permute-start(f32[8,1536]{1,0:T(8,128)S(1)} %fusion), channel_id=1, source_target_pairs={{0,17},{1,18},{2,19},{3,20},{4,21},{5,22},{6,23},{7,24},{8,25},{9,... | collective-permute-start | bytes 147464
  1356.3 69.6 %collective-permute-start.15 = (f32[8,1536]{1,0:T(8,128)S(1)}, f32[8,1536]{1,0:T(8,128)S(1)}, u32[]{:S(2)}, u32[]{:S(2)}) collective-permute-start(f32[8,1536]{1,0:T(8,128)S(1)} %fusion), channel_id=1, source_target_pairs={{0,16},{1,17},{2,18},{3,19},{4,20},{5,21},{6,22},{7,23},{8,24},{9,... | collective-permute-start | bytes 147464
  1373.2 81.4 %collective-permute-start.14 = (f32[8,1536]{1,0:T(8,128)S(1)}, f32[8,1536]{1,0:T(8,128)S(1)}, u32[]{:S(2)}, u32[]{:S(2)}) collective-permute-start(f32[8,1536]{1,0:T(8,128)S(1)} %fusion), channel_id=1, source_target_pairs={{0,15},{1,16},{2,17},{3,18},{4,19},{5,20},{6,21},{7,22},{8,23},{9,... | collective-permute-start | bytes 147464
  1386.4 80.7 %collective-permute-start.13 = (f32[8,1536]{1,0:T(8,128)S(1)}, f32[8,1536]{1,0:T(8,128)S(1)}, u32[]{:S(2)}, u32[]{:S(2)}) collective-permute-start(f32[8,1536]{1,0:T(8,128)S(1)} %fusion), channel_id=1, source_target_pairs={{0,14},{1,15},{2,16},{3,17},{4,18},{5,19},{6,20},{7,21},{8,22},{9,... | collective-permute-start | bytes 147464
  1399.5 80.7 %collective-permute-start.12 = (f32[8,1536]{1,0:T(8,128)S(1)}, f32[8,1536]{1,0:T(8,128)S(1)}, u32[]{:S(2)}, u32[]{:S(2)}) collective-permute-start(f32[8,1536]{1,0:T(8,128)S(1)} %fusion), channel_id=1, source_target_pairs={{0,13},{1,14},{2,15},{3,16},{4,17},{5,18},{6,19},{7,20},{8,21},{9,... | collective-permute-start | bytes 147464
  1412.7 80.7 %collective-permute-start.11 = (f32[8,1536]{1,0:T(8,128)S(1)}, f32[8,1536]{1,0:T(8,128)S(1)}, u32[]{:S(2)}, u32[]{:S(2)}) collective-permute-start(f32[8,1536]{1,0:T(8,128)S(1)} %fusion), channel_id=1, source_target_pairs={{0,12},{1,13},{2,14},{3,15},{4,16},{5,17},{6,18},{7,19},{8,20},{9,... | collective-permute-start | bytes 147464
  1425.8 80.7 %collective-permute-start.10 = (f32[8,1536]{1,0:T(8,128)S(1)}, f32[8,1536]{1,0:T(8,128)S(1)}, u32[]{:S(2)}, u32[]{:S(2)}) collective-permute-start(f32[8,1536]{1,0:T(8,128)S(1)} %fusion), channel_id=1, source_target_pairs={{0,11},{1,12},{2,13},{3,14},{4,15},{5,16},{6,17},{7,18},{8,19},{9,... | collective-permute-start | bytes 147464
  1439.0 258.6 %all-to-all-start.12 = ((bf16[32,2,6144]{2,1,0:T(2,128)(2,1)}), bf16[32,2,6144]{2,1,0:T(2,128)(2,1)S(1)}, u32[]{:S(2)}, u32[]{:S(2)}) async-start(bf16[32,2,6144]{2,1,0:T(2,128)(2,1)} %reshape.576), calls=%async_computation.12 | async-start | bytes 1572864 | tf_op jit(solution)/shard_map/all_to_all | solution.py:149
  1454.6 66.4 %collective-permute-start.9 = (f32[8,1536]{1,0:T(8,128)S(1)}, f32[8,1536]{1,0:T(8,128)S(1)}, u32[]{:S(2)}, u32[]{:S(2)}) collective-permute-start(f32[8,1536]{1,0:T(8,128)S(1)} %fusion), channel_id=1, source_target_pairs={{0,10},{1,11},{2,12},{3,13},{4,14},{5,15},{6,16},{7,17},{8,18},{9,... | collective-permute-start | bytes 147464
  1467.2 67.0 %collective-permute-start.8 = (f32[8,1536]{1,0:T(8,128)S(1)}, f32[8,1536]{1,0:T(8,128)S(1)}, u32[]{:S(2)}, u32[]{:S(2)}) collective-permute-start(f32[8,1536]{1,0:T(8,128)S(1)} %fusion), channel_id=1, source_target_pairs={{0,9},{1,10},{2,11},{3,12},{4,13},{5,14},{6,15},{7,16},{8,17},{9,1... | collective-permute-start | bytes 147464
  1480.3 67.0 %collective-permute-start.7 = (f32[8,1536]{1,0:T(8,128)S(1)}, f32[8,1536]{1,0:T(8,128)S(1)}, u32[]{:S(2)}, u32[]{:S(2)}) collective-permute-start(f32[8,1536]{1,0:T(8,128)S(1)} %fusion), channel_id=1, source_target_pairs={{0,8},{1,9},{2,10},{3,11},{4,12},{5,13},{6,14},{7,15},{8,16},{9,17... | collective-permute-start | bytes 147464
  1493.5 67.0 %collective-permute-start.6 = (f32[8,1536]{1,0:T(8,128)S(1)}, f32[8,1536]{1,0:T(8,128)S(1)}, u32[]{:S(2)}, u32[]{:S(2)}) collective-permute-start(f32[8,1536]{1,0:T(8,128)S(1)} %fusion), channel_id=1, source_target_pairs={{0,7},{1,8},{2,9},{3,10},{4,11},{5,12},{6,13},{7,14},{8,15},{9,16}... | collective-permute-start | bytes 147464
  1507.2 66.4 %collective-permute-start.5 = (f32[8,1536]{1,0:T(8,128)S(1)}, f32[8,1536]{1,0:T(8,128)S(1)}, u32[]{:S(2)}, u32[]{:S(2)}) collective-permute-start(f32[8,1536]{1,0:T(8,128)S(1)} %fusion), channel_id=1, source_target_pairs={{0,6},{1,7},{2,8},{3,9},{4,10},{5,11},{6,12},{7,13},{8,14},{9,15},... | collective-permute-start | bytes 147464
  1521.1 73.9 %collective-permute-start.4 = (f32[8,1536]{1,0:T(8,128)S(1)}, f32[8,1536]{1,0:T(8,128)}, u32[]{:S(2)}, u32[]{:S(2)}) collective-permute-start(f32[8,1536]{1,0:T(8,128)S(1)} %fusion), channel_id=1, source_target_pairs={{0,5},{1,6},{2,7},{3,8},{4,9},{5,10},{6,11},{7,12},{8,13},{9,14},{... | collective-permute-start | bytes 147464
  (171 other events, 4393.6 us)
Sparse Core Ops, SparseCore 0:
  11.9 122.9 all-gather.2
where the time goes:
time: 1730 us; the launch traced here: 1710 us
  blocking collectives  647 us (37%)
  starting transfers between devices  634 us (37%)
  local copies, waits for them, and re-layouts  197 us (11%)
  waiting for transfers between devices  120 us (7%)
  matrix products  63.1 us (4%)
  other arithmetic  31.6 us (2%)
  between operations  17.3 us (1%)
    unnamed x1, blocking collectives  647 us
    unnamed x64, starting transfers between devices  533 us
    unnamed x277, local copies, waits for them, and re-layouts  139 us
  transfers between devices with their start and end apart: 79, of which 15 were waited for; matrix products, arithmetic and copies ran while one was open for 14% of the time, Pallas kernels for 0%

commit v1 on v0

v1 whole, which is shorter than its diff:
```python
import functools
import math

import jax
import jax.numpy as jnp
from jax import lax
from jax.experimental import pallas as pl
from jax.experimental.pallas import tpu as pltpu
from jax.sharding import PartitionSpec as P

HD = 64
PAIR = 2 * HD
NX, NC, NY, NZ = 4, 2, 4, 8
NS = NY * NZ
TILES = 256
WIDTH = 1536
EACH = TILES // NS
PAIRS = WIDTH // PAIR
CH = 2
CW = WIDTH // CH
HW = CW // 2
CP = PAIRS // CH
LINE = WIDTH // (NX * NC)
BLOCK = LINE // NY
ROWS = BLOCK // NZ
LOG2E = 1.4426950408889634
SCALE = HD**-0.5
NONE = -1e30
FLOOR = -1e29
MESH = pl.DeviceIdType.MESH
F32 = jnp.float32
BF16 = jnp.bfloat16
A_QK, A_V, A_D, A_O, A_G, A_GV = (CH * n for n in range(6))
A_F, A_L, A_S = 6 * CH, 6 * CH + 1, 6 * CH + 2
A_ALL = 6 * CH + 3


def nt(a, b):
    return lax.dot_general(a, b, (((1,), (1,)), ((), ())), preferred_element_type=F32)


def nn(a, b):
    return lax.dot_general(a, b, (((1,), (0,)), ((), ())), preferred_element_type=F32)


def tn(a, b):
    return lax.dot_general(a, b, (((0,), (0,)), ((), ())), preferred_element_type=F32)


def exact(a, b):
    return lax.dot_general(
        a, b, (((1,), (0,)), ((), ())), precision=lax.Precision.HIGHEST, preferred_element_type=F32
    )


def iota(shape, axis):
    return lax.broadcasted_iota(jnp.int32, shape, axis)


def halves():
    low = (iota((1, PAIR), 1) < HD).astype(F32)
    return low.astype(BF16), (1.0 - low).astype(BF16)


def joined(a, b):
    shape = (NS, EACH, a.shape[1])
    both = [a.astype(F32).reshape(shape), b.astype(F32).reshape(shape)]
    return jnp.concatenate(both, axis=1).astype(BF16)


def parted(block):
    wide = block.astype(F32)
    shape = (TILES, block.shape[2])
    return wide[:, :EACH].reshape(shape).astype(BF16), wide[:, EACH:].reshape(shape).astype(BF16)


def pair_at(p):
    return pl.ds(pl.multiple_of(p * PAIR, PAIR), PAIR)


def forward_pair(q, k, v, masked):
    ones = halves()
    tops, sums = [], []
    for e in range(2):
        scores = masked(e, nt(q * ones[e], k) * (SCALE * LOG2E))
        top = jnp.maximum(jnp.max(scores, axis=1, keepdims=True), FLOOR)
        weights = jnp.exp2(scores - top).astype(BF16)
        tops.append(top)
        sums.append(nn(weights, v * ones[e] + ones[1 - e]))
    low = iota((TILES, PAIR), 1) < HD
    total = pltpu.roll(jnp.where(low, sums[1], sums[0]), HD, 1)
    total = jnp.maximum(total, 1e-30)
    out = jnp.where(low, sums[0], sums[1]) / total
    lse = jnp.where(low, tops[0], tops[1]) + jnp.log(total) * LOG2E
    return out, lse


def backward_pair(q, k, v, d, masked, lse, delta):
    ones = halves()
    gq = gk = gv = None
    for e in range(2):
        qe, de, ke = q * ones[e], d * ones[e], k * ones[e]
        probs = masked(e, nt(k, qe) * (SCALE * LOG2E) - lse[e])
        dscore = (probs * (nt(v, de) - delta[e])).astype(BF16)
        terms = (tn(dscore, ke), nn(dscore, qe), nn(probs.astype(BF16), de))
        gq, gk, gv = terms if e == 0 else (gq + terms[0], gk + terms[1], gv + terms[2])
    return gq * SCALE, gk * SCALE, gv


def remote(src, dst, send, recv, peer):
    return pltpu.make_async_remote_copy(
        src_ref=src, dst_ref=dst, send_sem=send, recv_sem=recv, device_id=peer, device_id_type=MESH
    )


def kernel(
    factor,
    q_in, k_in, v_in, g_in, keep_in, seg, dil, w_in,
    out_lo, out_q, out_k, out_v, out_w,
    qp, kp, vp, gp, dp, qf, kf, vf, df, of, o_near, attn, attn_t, nq, nk, nv,
    x_fwd, x_bwd, stat, stat_t, far_t, bias_row, bias_col,
    qk_s, v_s, d_s, qk_r, v_r, d_r, o_r, g_r, gv_r,
    f_s, f_r, l_s, l_r, s_s, s_r,
    w_src, w_z, w_full,
    c_s, c_r, own, x_s, x_r, y_s, y_r, z_s, z_r,
    a_send, a_recv, w_send, wz_recv, wy_recv, wx_recv, wc_recv,
    r_send, rc_recv, rx_recv, ry_recv, rz_recv,
):
    slide = lax.axis_index("slide")
    me = lax.axis_index("seq")
    x, c = lax.div(slide, NC), lax.rem(slide, NC)
    y, z = lax.div(me, NZ), lax.rem(me, NZ)

    def device(xx, cc, yy, zz):
        return (xx * NC + cc, yy * NZ + zz)

    def peer_of(n):
        return lax.rem(y + lax.div(n, NZ), NY) * NZ + lax.rem(z + lax.rem(n, NZ), NZ)

    sibling = device(x, 1 - c, y, z)
    barrier = pltpu.get_barrier_semaphore()

    def greet(n, carry):
        pl.semaphore_signal(barrier, inc=1, device_id=(slide, peer_of(n)), device_id_type=MESH)
        return carry

    lax.fori_loop(1, NS, greet, 0)
    for peer in [sibling] + [device(lax.rem(x + step, NX), c, y, z) for step in range(1, NX)]:
        pl.semaphore_signal(barrier, inc=1, device_id=peer, device_id_type=MESH)
    pl.semaphore_wait(barrier, NS - 1 + NX)

    def exchange(src, dst, k):
        def body(n, carry):
            peer = peer_of(n)
            remote(src.at[peer], dst.at[me], a_send.at[k], a_recv.at[k], (slide, peer)).start()
            return carry

        lax.fori_loop(1, NS, body, 0)
        dst.at[me][...] = src.at[me][...]

    def arrived(dst, k):
        part = dst.at[pl.ds(0, NS - 1)]
        pltpu.make_async_copy(part, part, a_recv.at[k]).wait()

    def departed(src, k):
        part = src.at[pl.ds(0, NS - 1)]
        pltpu.make_async_copy(part, part, a_send.at[k]).wait()

    w_started, r_started = [], []

    def send_w(src, dst, recv, peer):
        copy = remote(src, dst, w_send.at[len(w_started)], recv, peer)
        copy.start()
        w_started.append(copy)
        return copy

    def send_r(src, dst, recv, peer):
        copy = remote(src, dst, r_send.at[len(r_started)], recv, peer)
        copy.start()
        r_started.append(copy)
        return copy

    def line_of(xx, cc):
        return pl.ds(pl.multiple_of((xx * NC + cc) * LINE, 16), LINE)

    w_src[...] = jnp.zeros_like(w_src)
    w_src[0:ROWS, :] = w_in[...]
    w_z[z] = w_src[...]
    wz = [
        send_w(w_src, w_z.at[z], wz_recv.at[step - 1], device(x, c, y, lax.rem(z + step, NZ)))
        for step in range(1, NZ)
    ]

    square = (TILES, TILES)
    line, lane = iota(square, 0), iota(square, 1)
    order = (lane == lax.rem(line, EACH) * NS + lax.div(line, EACH)).astype(F32).astype(BF16)
    back = (lane == lax.rem(line, NS) * EACH + lax.div(line, NS)).astype(F32).astype(BF16)
    for ch in range(CH):
        cols = pl.ds(ch * CW, CW)
        q = nn(order, q_in[:, cols])
        k = nn(order, k_in[:, cols])
        qk_s[ch] = joined(q, k)
        exchange(qk_s.at[ch], qk_r.at[ch], A_QK + ch)
        qp[:, cols] = q.astype(BF16)
        kp[:, cols] = k.astype(BF16)
        v = nn(order, v_in[:, cols])
        v_s[ch] = joined(v[:, :HW], v[:, HW:])
        exchange(v_s.at[ch], v_r.at[ch], A_V + ch)
        vp[:, cols] = v.astype(BF16)
        if ch == 0:
            keep = keep_in[...].astype(F32).astype(BF16)
            keep_cols = nt(order, jnp.broadcast_to(keep, (PAIR, TILES)))
            f_s[...] = keep_cols.reshape(NS, EACH, PAIR)
            exchange(f_s, f_r, A_F)
    for ch in range(CH):
        cols = pl.ds(ch * CW, CW)
        gp[:, cols] = nn(order, g_in[:, cols]).astype(BF16)

    keep_row = nt(jnp.broadcast_to(keep, (16, TILES)), order)[0:1]
    pos_l = lax.rem(line, EACH) * NS + lax.div(line, EACH)
    pos_c = lax.rem(lane, EACH) * NS + lax.div(lane, EACH)
    apart = lax.bitwise_xor(pos_l, pos_c)
    same = line == lane
    x_fwd[...] = jnp.where(same, 0, apart + jnp.where(keep_row > 0.5, 0, 65536))
    keep_wide = jnp.concatenate([keep_cols, keep_cols], axis=1)
    x_bwd[...] = jnp.where(same, 0, apart + jnp.where(keep_wide > 0.5, 0, 65536))

    def bits(p, e):
        head = 2 * p + e
        return 65536 + (TILES - seg[head]) + (dil[head] - 1)

    for copy in wz:
        copy.wait_recv()
    out_row = iota((BLOCK, NZ * 16), 0)
    in_row = iota((BLOCK, NZ * 16), 1)
    pick = (in_row == lax.div(out_row, ROWS) * 16 + lax.rem(out_row, ROWS)).astype(F32).astype(BF16)
    mine = pl.ds(pl.multiple_of(((x * NC + c) * NY + y) * BLOCK, 16), BLOCK)
    w_full[mine, :] = nn(pick, w_z[...].reshape(NZ * 16, WIDTH)).astype(BF16)
    wy = [
        send_w(w_full.at[mine], w_full.at[mine], wy_recv.at[step - 1], device(x, c, lax.rem(y + step, NY), z))
        for step in range(1, NY)
    ]

    def put_stat(p, stats, values):
        return jnp.where(lax.rem(iota((TILES, PAIR), 1), HD) == p, values, stats)

    def near_forward(p, stats):
        at = pair_at(p)

        def masked(e, scores):
            return jnp.where(lax.bitwise_and(x_fwd[...], bits(p, e)) == 0, scores, NONE)

        out, lse = forward_pair(qp[:, at], kp[:, at], vp[:, at], masked)
        o_near[:, at] = out
        return put_stat(p, stats, lse)

    near_lse = lax.fori_loop(0, 3, near_forward, jnp.zeros((TILES, PAIR), F32))

    for copy in wy:
        copy.wait_recv()
    mine = line_of(x, c)
    wx = [
        send_w(w_full.at[mine], w_full.at[mine], wx_recv.at[step - 1], device(lax.rem(x + step, NX), c, y, z))
        for step in range(1, NX)
    ]
    wc = [send_w(w_full.at[mine], w_full.at[mine], wc_recv.at[0], sibling)]
    near_lse = lax.fori_loop(3, PAIRS, near_forward, near_lse)
    stat[...] = near_lse

    arrived(f_r, A_F)
    flags = f_r[...].reshape(TILES, PAIR)
    bias = jnp.where(flags > 0.5, 0.0, NONE)
    bias_col[...] = jnp.concatenate([bias, bias], axis=1)
    bias_row[...] = jnp.transpose(bias)[0:8]

    def far_forward(p, stats):
        at = pair_at(p)
        out, lse = forward_pair(
            qf[:, at], kf[:, at], vf[:, at], lambda e, scores: scores + bias_row[0:1, :]
        )
        of[:, at] = out.astype(BF16)
        return put_stat(p, stats, lse)

    far_lse = jnp.zeros((TILES, PAIR), F32)
    for ch in range(CH):
        cols, low, high = pl.ds(ch * CW, CW), pl.ds(ch * CW, HW), pl.ds(ch * CW + HW, HW)
        arrived(qk_r.at[ch], A_QK + ch)
        qf[:, cols], kf[:, cols] = parted(qk_r[ch])
        arrived(v_r.at[ch], A_V + ch)
        vf[:, low], vf[:, high] = parted(v_r[ch])
        far_lse = lax.fori_loop(ch * CP, (ch + 1) * CP, far_forward, far_lse)
        departed(v_s.at[ch], A_V + ch)
        v_s[ch] = joined(of[:, low], of[:, high])
        exchange(v_s.at[ch], o_r.at[ch], A_O + ch)
    l_s[...] = far_lse.reshape(NS, EACH, PAIR)
    exchange(l_s, l_r, A_L)

    for step in range(1, NX):
        wx[step - 1].wait_recv()
        there = line_of(lax.rem(x + NX - step, NX), c)
        wc.append(send_w(w_full.at[there], w_full.at[there], wc_recv.at[step], sibling))
    for copy in wc:
        copy.wait_recv()
    for ch in range(CH):
        for half in range(2):
            cols = pl.ds(ch * CW + half * HW, HW)
            dp[:, cols] = nt(gp[...], w_full[cols, :]).astype(BF16)
        low, high = pl.ds(ch * CW, HW), pl.ds(ch * CW + HW, HW)
        d_s[ch] = joined(dp[:, low], dp[:, high])
        exchange(d_s.at[ch], d_r.at[ch], A_D + ch)

    arrived(l_r, A_L)
    lse_near = stat[...]
    lse_far = l_r[...].reshape(TILES, PAIR)
    top = jnp.maximum(lse_near, lse_far)
    lse = top + jnp.log(jnp.exp2(lse_near - top) + jnp.exp2(lse_far - top)) * LOG2E
    share_near = jnp.exp2(lse_near - lse)
    share_far = jnp.exp2(lse_far - lse)
    for ch in range(CH):
        low, high = pl.ds(ch * CW, HW), pl.ds(ch * CW + HW, HW)
        arrived(o_r.at[ch], A_O + ch)
        of[:, low], of[:, high] = parted(o_r[ch])

    def combine(p, delta):
        at = pair_at(p)
        small = (PAIR, PAIR)
        first, second = iota(small, 0), iota(small, 1)
        together = (first < HD) == (second < HD)
        spread = (together & (lax.rem(first, HD) == p)).astype(F32)
        gather = (together & (lax.rem(second, HD) == p + 16)).astype(F32)
        whole = exact(share_near, spread) * o_near[:, at] + exact(share_far, spread) * of[:, at].astype(F32)
        attn[:, at] = whole.astype(BF16)
        attn_t[at, :] = jnp.transpose(whole).astype(BF16)
        return delta + exact(whole * dp[:, at].astype(F32), gather)

    delta = lax.fori_loop(0, PAIRS, combine, jnp.zeros((TILES, PAIR), F32))
    stats = jnp.where(lax.rem(iota((TILES, PAIR), 1), HD) < 16, lse, delta)
    s_s[...] = stats.reshape(NS, EACH, PAIR)
    exchange(s_s, s_r, A_S)
    stat_t[...] = jnp.transpose(stats)

    for step in range(NX):
        to = lax.rem(x + step + 1, NX)
        c_s[step] = nn(attn_t[line_of(to, 1 - c), :], gp[...]).astype(BF16)
        send_r(c_s.at[step], c_r.at[step], rc_recv.at[step], sibling)

    def rows_of(table, p):
        lse = [table[pl.ds(p + HD * e, 1), :] for e in range(2)]
        delta = [table[pl.ds(p + HD * e + 16, 1), :] for e in range(2)]
        return lse, delta

    arrived(s_r, A_S)
    far_t[...] = jnp.transpose(s_r[...].reshape(TILES, PAIR))

    def far_backward(ch, p, carry):
        at = pair_at(p)
        here = pair_at(p - ch * CP)
        gq, gk, gv = backward_pair(
            qf[:, at], kf[:, at], vf[:, at], df[:, at],
            lambda e, scores: jnp.exp2(scores + bias_col[...]), *rows_of(far_t, p),
        )
        qk_s[ch, :, :, here] = joined(gq, gk)
        of[:, at] = gv.astype(BF16)
        return carry

    for ch in range(CH):
        low, high = pl.ds(ch * CW, HW), pl.ds(ch * CW + HW, HW)
        arrived(d_r.at[ch], A_D + ch)
        df[:, low], df[:, high] = parted(d_r[ch])
        departed(qk_s.at[ch], A_QK + ch)
        lax.fori_loop(ch * CP, (ch + 1) * CP, functools.partial(far_backward, ch), 0)
        exchange(qk_s.at[ch], g_r.at[ch], A_G + ch)
        departed(d_s.at[ch], A_D + ch)
        d_s[ch] = joined(of[:, low], of[:, high])
        exchange(d_s.at[ch], gv_r.at[ch], A_GV + ch)

    ahead = []
    for step in range(NX):
        to = lax.rem(x + step + 1, NX)
        r_started[step].wait_recv()
        total = nn(attn_t[line_of(to, c), :], gp[...]) + c_r[step].astype(F32)
        if step < NX - 1:
            x_s[step] = total.astype(BF16)
            ahead.append(send_r(x_s.at[step], x_r.at[step], rx_recv.at[step], device(to, c, y, z)))
        else:
            own[...] = total

    def near_backward(p, carry):
        at = pair_at(p)

        def masked(e, scores):
            return jnp.where(lax.bitwise_and(x_bwd[...], bits(p, e)) == 0, jnp.exp2(scores), 0.0)

        nq[:, at], nk[:, at], nv[:, at] = backward_pair(
            qp[:, at], kp[:, at], vp[:, at], dp[:, at], masked, *rows_of(stat_t, p)
        )
        return carry

    lax.fori_loop(0, PAIRS // 2, near_backward, 0)
    for copy in ahead:
        copy.wait_recv()
    total = own[...]
    for step in range(NX - 1):
        total = total + x_r[step].astype(F32)
    y_s[...] = total.reshape(NY, BLOCK, WIDTH)
    ahead = []
    for step in range(NY - 1):
        to = lax.rem(y + step + 1, NY)
        ahead.append(send_r(y_s.at[to], y_r.at[step], ry_recv.at[step], device(x, c, to, z)))
    lax.fori_loop(PAIRS // 2, PAIRS, near_backward, 0)
    for copy in ahead:
        copy.wait_recv()
    total = y_s[y]
    for step in range(NY - 1):
        total = total + y_r[step]
    z_s[...] = jnp.zeros_like(z_s)
    for step in range(NZ):
        z_s[step, 0:ROWS, :] = total[step * ROWS : (step + 1) * ROWS]
    ahead = []
    for step in range(NZ - 1):
        to = lax.rem(z + step + 1, NZ)
        ahead.append(send_r(z_s.at[to], z_r.at[step], rz_recv.at[step], device(x, c, y, to)))

    for ch in range(CH):
        cols = pl.ds(ch * CW, CW)
        done = nn(attn[...], w_full[:, cols]).astype(BF16)
        out_lo[:, cols] = nn(back, done).astype(BF16)

    for ch in range(CH):
        cols, low, high = pl.ds(ch * CW, CW), pl.ds(ch * CW, HW), pl.ds(ch * CW + HW, HW)
        arrived(g_r.at[ch], A_G + ch)
        far_q, far_k = parted(g_r[ch])
        out_q[:, cols] = nn(back, (nq[:, cols] + far_q.astype(F32)).astype(BF16)).astype(BF16)
        out_k[:, cols] = nn(back, (nk[:, cols] + far_k.astype(F32)).astype(BF16)).astype(BF16)
        arrived(gv_r.at[ch], A_GV + ch)
        far_low, far_high = parted(gv_r[ch])
        out_v[:, low] = nn(back, (nv[:, low] + far_low.astype(F32)).astype(BF16)).astype(BF16)
        out_v[:, high] = nn(back, (nv[:, high] + far_high.astype(F32)).astype(BF16)).astype(BF16)

    for copy in ahead:
        copy.wait_recv()
    total = z_s[z]
    for step in range(NZ - 1):
        total = total + z_r[step]
    out_w[...] = total[0:ROWS] * factor
    for copy in w_started + r_started:
        copy.wait_send()
    for ch in range(CH):
        departed(v_s.at[ch], A_O + ch)
        departed(qk_s.at[ch], A_G + ch)
        departed(d_s.at[ch], A_GV + ch)
    departed(f_s, A_F)
    departed(l_s, A_L)
    departed(s_s, A_S)


def layer(queries, key_rows, value_rows, tissue, segment_len, dilation, out_weight, grad_out):
    shape = (TILES, WIDTH)
    vmem = pl.BlockSpec(memory_space=pltpu.VMEM)
    smem = pl.BlockSpec(memory_space=pltpu.SMEM)
    low, wide = pltpu.VMEM(shape, BF16), pltpu.VMEM(shape, F32)
    stats = pltpu.VMEM((NS, EACH, PAIR), F32)
    table = pltpu.VMEM((PAIR, TILES), F32)
    square = pltpu.VMEM((TILES, TILES), jnp.int32)
    both = pltpu.VMEM((CH, NS, 2 * EACH, CW), BF16)
    single = pltpu.VMEM((CH, NS, 2 * EACH, HW), BF16)
    dma = pltpu.SemaphoreType.DMA
    factor = 1.0 / math.sqrt(NX * NC * NS * TILES)
    outs = pl.pallas_call(
        functools.partial(kernel, factor),
        out_shape=[jax.ShapeDtypeStruct(shape, BF16)] * 4 + [jax.ShapeDtypeStruct((ROWS, WIDTH), F32)],
        in_specs=[vmem] * 5 + [smem] * 2 + [vmem],
        out_specs=[vmem] * 5,
        scratch_shapes=[low] * 10 + [wide] + [low, pltpu.VMEM((WIDTH, TILES), BF16)] + [wide] * 3
        + [square] * 2 + [pltpu.VMEM((TILES, PAIR), F32), table, table]
        + [pltpu.VMEM((8, TILES), F32), pltpu.VMEM((TILES, TILES), F32)]
        + [both, single, single, both, single, single, single, both, single]
        + [stats] * 6
        + [
            pltpu.VMEM((16, WIDTH), BF16),
            pltpu.VMEM((NZ, 16, WIDTH), BF16),
            pltpu.VMEM((WIDTH, WIDTH), BF16),
            pltpu.VMEM((NX, LINE, WIDTH), BF16),
            pltpu.VMEM((NX, LINE, WIDTH), BF16),
            pltpu.VMEM((LINE, WIDTH), F32),
            pltpu.VMEM((NX - 1, LINE, WIDTH), BF16),
            pltpu.VMEM((NX - 1, LINE, WIDTH), BF16),
            pltpu.VMEM((NY, BLOCK, WIDTH), F32),
            pltpu.VMEM((NY - 1, BLOCK, WIDTH), F32),
            pltpu.VMEM((NZ, 8, WIDTH), F32),
            pltpu.VMEM((NZ - 1, 8, WIDTH), F32),
            dma((A_ALL,)),
            dma((A_ALL,)),
            dma((NZ + NY + 2 * NX,)),
            dma((NZ,)),
            dma((NY,)),
            dma((NX,)),
            dma((NX,)),
            dma((NZ + NY + 2 * NX,)),
            dma((NX,)),
            dma((NX,)),
            dma((NY,)),
            dma((NZ,)),
        ],
        compiler_params=pltpu.CompilerParams(
            collective_id=0, has_side_effects=True, vmem_limit_bytes=60 * 1024 * 1024
        ),
    )(
        queries[0], key_rows[0], value_rows[0], grad_out[0], tissue, segment_len, dilation, out_weight
    )
    return tuple(out[None] for out in outs[:4]) + (outs[4],)


def solution(mesh):
    tiles = P("slide", "seq", None)
    rows = P(("slide", "seq"), None)
    return jax.shard_map(
        layer,
        mesh=mesh,
        in_specs=(tiles, tiles, tiles, P("slide", "seq"), P(), P(), rows, tiles),
        out_specs=(tiles, tiles, tiles, tiles, rows),
        check_vma=False,
    )
```

time: 1730 us -> 199 us (0.12); the launches traced: 1710 us -> 197 us
  blocking collectives: 647 us -> 0 us
  starting transfers between devices: 634 us -> 0 us
  local copies, waits for them, and re-layouts: 197 us -> 6.47 us
  Pallas kernels: 0 us -> 190 us
  waiting for transfers between devices: 120 us -> 0 us
  matrix products: 63.1 us -> 0 us
  other arithmetic: 31.6 us -> 0 us
    unnamed x1 -> x0, blocking collectives: 647 us -> none
    unnamed x64 -> x0, starting transfers between devices: 533 us -> none
    pallas_call x0 -> x1, Pallas kernels: none -> 190 us  [layer(): pl.pallas_call(functools.partial(kernel, factor), out_shape=[jax.ShapeDty...]
    unnamed x277 -> x13, local copies, waits for them, and re-layouts: 139 us -> 6.47 us
    all_to_all x14 -> x0, waiting for transfers between devices: 109 us -> none  [the longest x1 24.2 us: local(): lax.all_to_all(acc_far.reshape(rows, 1, features), 'seq', split_axis=0, c...]
    all_to_all x14 -> x0, starting transfers between devices: 101 us -> none  [the longest x1 12.5 us: local(): lax.all_to_all(to_rows(delta.T), 'seq', split_axis=1, concat_axis=0, tile...]
    dot_general x15 -> x0, matrix products: 63.1 us -> none  [the longest x2 13.4 us: backward_part(): jnp.einsum('ihd,jhd->hij', d_heads, v_heads, preferred_element_type=jnp.f...]
    another operation x13 -> x0, local copies, waits for them, and re-layouts: 30 us -> none  [the longest x8 17.1 us: heads_of(): return matrix.reshape(matrix.shape[0], matrix.shape[1] // HD, HD)]
  transfers between devices with their start and end apart: 79 -> 0, of which waited for: 15 -> 0; matrix products, arithmetic and copies ran while one was open for 14% -> 0% of each run, Pallas kernels for 0% -> 0%
where the time goes in v1:
time: 199 us; the launch traced here: 197 us
  Pallas kernels  190 us (95%)
  local copies, waits for them, and re-layouts  6.47 us (3%)
    pallas_call x1, Pallas kernels, layer(): pl.pallas_call(functools.partial(kernel, factor), out_shape=[jax.ShapeDty...  190 us
    unnamed x13, local copies, waits for them, and re-layouts  6.47 us

profile of v1, /device:TPU:2, one launch (start us, length us, event | category | flops | bytes accessed | tf_op | source)
XLA Modules:
  0.0 197.2 jit_solution(1462232535179505557)
XLA Ops:
  0.6 190.1 %shard_map.119 = (bf16[256,1536]{1,0:T(8,128)(2,1)}, bf16[256,1536]{1,0:T(8,128)(2,1)}, bf16[256,1536]{1,0:T(8,128)(2,1)}, bf16[256,1536]{1,0:T(8,128)(2,1)}, f32[6,1536]{1,0:T(8,128)}) custom-call(bf16[256,1536]{1,0:T(8,128)(2,1)} %bitcast.12, bf16[256,1536]{1,0:T(8,128)(2,1)} %bitcast.13, bf16[256,1536]{1,0:T(8,128)(2,1)} %bitcast.14, ...), custom_call_target="tpu_custom_call" | custom-call | tf_op jit(solution)/shard_map/pallas_call | solution.py:469
  190.7 0.0 copy-start.2
  190.7 2.1 %copy.18 = bf16[1,256,1536]{2,1,0:T(8,128)(2,1)} copy(bf16[1,256,1536]{2,1,0:T(8,128)(2,1)} %bitcast.11) | data formatting | bytes 1572864
  192.9 0.0 copy-done.2
  192.9 0.0 copy-start.1
  192.9 0.9 copy.19
  193.7 0.5 copy-done.1
  194.3 0.0 copy-start
  194.3 0.9 copy.20
  195.2 0.5 copy-done
  195.7 0.0 copy-start.3
  195.7 0.9 copy.21
  196.6 0.0 copy-done.3
  196.6 0.6 copy.22
Async XLA Ops:
  190.7 2.1 %copy-start.2 = (bf16[256,1536]{1,0:T(8,128)(2,1)S(1)}, bf16[256,1536]{1,0:T(8,128)(2,1)}, u32[]{:S(2)}) copy-start(bf16[256,1536]{1,0:T(8,128)(2,1)} %get-tuple-element.11) | copy-start | bytes 2359300
  192.9 1.4 copy-start.1
  194.3 1.4 copy-start
  195.7 0.9 copy-start.3
